TPU v7x, 32 devices: a whole 2x2x4 slice. The times are simulated.
32 devices in a mesh: section: 4 (over z), tm: 4 (over y, x), batch: 2 (over core).
Axes of the slice: x: 2, y: 2, z: 4, core: 2. Of those that a mesh axis runs over, the one named last changes fastest.
Arguments:
- acts: bfloat16 [4, 4, 8, 6, 10240], P('section', 'batch', 'tm'), may hold values from -6 to 6
- cot: bfloat16 [4, 8, 6, 10240], P('batch', 'tm'), may hold values from -6 to 6
- spatial_weight: bfloat16 [4, 9, 64, 64], P('section'), may hold values from -0.25 to 0.25
- temporal_weight: bfloat16 [4, 3, 64, 64], P('section'), may hold values from -0.4375 to 0.4375
Outputs:
- grad_in: bfloat16 [4, 4, 8, 6, 10240], P('section', 'batch', 'tm')
- grad_spatial: float32 [4, 9, 64, 64], P('section')
- grad_temporal: float32 [4, 3, 64, 64], P('section')
All inputs are finite; a program needn't handle non-finite values.
Results may differ from a plain program's by a relative error of at most 0.012.
Values may be sent and summed in bfloat16 or wider, within the bound.
A program may use at most 128 MiB of HBM per device.

v0:
```python
import jax
import jax.numpy as jnp
from jax import lax
from jax.sharding import PartitionSpec as P

TIME_DILATION = 2


def from_behind(value, axis, steps):
    count = lax.axis_size(axis)
    first, last = (max(0, -steps), min(count, count - steps))
    return lax.ppermute(value, axis, [(source, source + steps) for source in range(first, last)])


def split_pixels(a, chans):
    return a.reshape(a.shape[:-1] + (a.shape[-1] // chans, chans))


def paired_kernel(kernel):
    return jnp.kron(jnp.eye(2, dtype=kernel.dtype), kernel)


def spatial_fwd(x, ws):
    rows, width = (x.shape[1], x.shape[2])
    chans = ws.shape[-1]
    padded = jnp.pad(x, ((0, 0), (1, 1), (chans, chans)))
    total = jnp.zeros(x.shape, jnp.float32)
    for i in range(3):
        for j in range(3):
            piece = split_pixels(padded[:, i : i + rows, j * chans : j * chans + width], 2 * chans)
            total = total + jnp.einsum(
                "nrpa,ab->nrpb",
                piece,
                paired_kernel(ws[3 * i + j]),
                preferred_element_type=jnp.float32,
            ).reshape(x.shape)
    return total


def spatial_back(gz, x, ws):
    rows, width = (x.shape[1], x.shape[2])
    chans = ws.shape[-1]
    xpad = jnp.pad(x, ((0, 0), (1, 1), (chans, chans)))
    gradient_padded = jnp.pad(gz, ((0, 0), (1, 1), (chans, chans)))
    gz_pairs = split_pixels(gz, 2 * chans)
    total = jnp.zeros(x.shape, jnp.float32)
    grads = []
    for i in range(3):
        for j in range(3):
            gpiece = split_pixels(
                gradient_padded[:, 2 - i : 2 - i + rows, (2 - j) * chans : (2 - j) * chans + width],
                2 * chans,
            )
            total = total + jnp.einsum(
                "nrpb,ab->nrpa",
                gpiece,
                paired_kernel(ws[3 * i + j]),
                preferred_element_type=jnp.float32,
            ).reshape(x.shape)
            xpiece = split_pixels(xpad[:, i : i + rows, j * chans : j * chans + width], 2 * chans)
            square = jnp.einsum(
                "nrpa,nrpb->ab", xpiece, gz_pairs, preferred_element_type=jnp.float32
            )
            grads.append(square[:chans, :chans] + square[chans:, chans:])
    return (total, jnp.stack(grads))


def temporal_back(h, gradient_piece, gradient_padded, dilation_step, wt):
    count = gradient_piece.shape[0]
    chans = wt.shape[-1]
    kernel_taps = [
        gradient_padded[2 * dilation_step : 2 * dilation_step + count],
        gradient_piece,
        gradient_padded[0:count],
    ]
    h_pix = split_pixels(h, chans)
    gh = jnp.zeros(gradient_piece.shape, jnp.float32)
    tgrads = []
    for k in range(3):
        tap = split_pixels(kernel_taps[k], chans)
        gh = gh + jnp.einsum(
            "trwd,cd->trwc", tap, wt[k], preferred_element_type=jnp.float32
        ).reshape(gradient_piece.shape)
        tgrads.append(jnp.einsum("trwc,trwd->cd", h_pix, tap, preferred_element_type=jnp.float32))
    return (gh.astype(jnp.bfloat16), jnp.stack(tgrads))


def section_backward(x, gradient_piece, ws, wt):
    dilation_step = TIME_DILATION
    z = spatial_fwd(x, ws)
    sig = jax.nn.sigmoid(z)
    h = (z * sig).astype(jnp.bfloat16)
    deriv = sig * (1.0 + z * (1.0 - sig))
    tile_gradient, h_tile = (
        lax.all_to_all(gradient_piece, "tm", split_axis=2, concat_axis=0, tiled=True),
        lax.all_to_all(h, "tm", split_axis=2, concat_axis=0, tiled=True),
    )
    gradient_padded = jnp.pad(tile_gradient, ((dilation_step, dilation_step), (0, 0), (0, 0)))
    gh_tile, tgrads = temporal_back(h_tile, tile_gradient, gradient_padded, dilation_step, wt)
    gh = lax.all_to_all(gh_tile, "tm", split_axis=0, concat_axis=2, tiled=True)
    gz = (gh.astype(jnp.float32) * deriv).astype(jnp.bfloat16)
    back, sgrads = spatial_back(gz, x, ws)
    result = (gradient_piece.astype(jnp.float32) + back).astype(jnp.bfloat16)
    return (result, sgrads, tgrads)


def body(acts, cot, spatial_weight, temporal_weight):
    section_idx = lax.axis_index("section")
    number_sections = lax.axis_size("section")
    micro = acts.shape[1]
    local_acts = acts[0]
    ws = spatial_weight[0]
    wt = temporal_weight[0]
    received = jnp.zeros(cot.shape[1:], jnp.bfloat16)
    grads_in = jnp.zeros(local_acts.shape, jnp.bfloat16)
    acc_spatial = jnp.zeros(ws.shape, jnp.float32)
    acc_temporal = jnp.zeros(wt.shape, jnp.float32)
    total_turns = micro + number_sections - 1
    for turn in range(total_turns):
        which = jnp.int32(turn) - (number_sections - 1 - section_idx)
        valid = jnp.logical_and(which >= 0, which < micro)
        clipped = jnp.clip(which, 0, micro - 1)
        x_now = lax.dynamic_index_in_dim(local_acts, clipped, 0, keepdims=False)
        top_grad = lax.dynamic_index_in_dim(cot, clipped, 0, keepdims=False)
        incoming = jnp.where(section_idx == number_sections - 1, top_grad, received)
        result, sgrads, tgrads = section_backward(x_now, incoming, ws, wt)
        weight = valid.astype(jnp.float32)
        acc_spatial = acc_spatial + weight * sgrads
        acc_temporal = acc_temporal + weight * tgrads
        select = (jnp.arange(micro, dtype=jnp.int32) == which)[:, None, None, None]
        grads_in = jnp.where(select, result[None], grads_in)
        if turn + 1 < total_turns:
            received = from_behind(result, "section", -1)
    sum_spatial, sum_temporal = lax.psum((acc_spatial, acc_temporal), ("tm", "batch"))
    return (grads_in[None], sum_spatial[None], sum_temporal[None])


def solution(mesh):
    in_specs = (
        P("section", "batch", "tm", None, None),
        P("batch", "tm", None, None),
        P("section", None, None, None),
        P("section", None, None, None),
    )
    out_specs = (
        P("section", "batch", "tm", None, None),
        P("section", None, None, None),
        P("section", None, None, None),
    )
    return jax.shard_map(body, mesh=mesh, in_specs=in_specs, out_specs=out_specs, check_vma=False)
```

profile of v0, /device:TPU:0, one launch (start us, length us, event | category | flops | bytes accessed | tf_op | source)
XLA Modules:
  0.0 927.0 jit_solution(14927379624928204376)
XLA Ops:
  127.6 13.6 %reshape.1686 = bf16[10240,2,6]{2,1,0:T(2,128)(2,1)} reshape(bf16[4,2,15360]{2,1,0:T(2,128)(2,1)} %all-to-all-done) | data formatting | bytes 491520
  141.2 10.6 %copy.624 = bf16[2,6,4,2560]{3,0,2,1:T(2,128)(2,1)S(1)} copy(bf16[2,6,4,2560]{1,0,3,2:T(2,128)(2,1)} %bitcast.1160) | data formatting | bytes 491520 | tf_op jit(solution)/shard_map/all_to_all | solution.py:95
  205.4 10.3 %copy.809 = bf16[2,6,10240]{1,0,2:T(2,128)(2,1)} copy(bf16[2,6,10240]{2,0,1:T(2,128)(2,1)} %get-tuple-element.11) | data formatting | bytes 491520 | tf_op jit(solution)/shard_map/convert_element_type | solution.py:92
  257.3 12.6 %reshape.1696 = bf16[10240,2,6]{2,1,0:T(2,128)(2,1)} reshape(bf16[4,2,15360]{2,1,0:T(2,128)(2,1)S(1)} %all-to-all-done.10) | data formatting | bytes 491520
  269.9 12.2 %copy.902 = bf16[2,6,4,2560]{3,2,0,1:T(4,128)(2,1)S(1)} copy(bf16[2,6,4,2560]{1,0,3,2:T(2,128)(2,1)} %bitcast.1162) | data formatting | bytes 491520 | tf_op jit(solution)/shard_map/all_to_all | solution.py:96
  283.5 12.6 %reshape.1688 = bf16[10240,2,6]{2,1,0:T(2,128)(2,1)} reshape(bf16[4,2,15360]{2,1,0:T(2,128)(2,1)S(1)} %all-to-all-done.2) | data formatting | bytes 491520
  296.2 10.2 %copy.652 = bf16[2,6,4,2560]{3,0,2,1:T(2,128)(2,1)S(1)} copy(bf16[2,6,4,2560]{1,0,3,2:T(2,128)(2,1)} %bitcast.1163) | data formatting | bytes 491520 | tf_op jit(solution)/shard_map/all_to_all | solution.py:95
  365.6 10.3 %copy.812 = bf16[2,6,10240]{1,0,2:T(2,128)(2,1)} copy(bf16[2,6,10240]{2,0,1:T(2,128)(2,1)} %get-tuple-element.9) | data formatting | bytes 491520 | tf_op jit(solution)/shard_map/convert_element_type | solution.py:92
  417.6 12.6 %reshape.1698 = bf16[10240,2,6]{2,1,0:T(2,128)(2,1)} reshape(bf16[4,2,15360]{2,1,0:T(2,128)(2,1)S(1)} %all-to-all-done.11) | data formatting | bytes 491520
  430.2 12.2 %copy.903 = bf16[2,6,4,2560]{3,2,0,1:T(4,128)(2,1)S(1)} copy(bf16[2,6,4,2560]{1,0,3,2:T(2,128)(2,1)} %bitcast.1165) | data formatting | bytes 491520 | tf_op jit(solution)/shard_map/all_to_all | solution.py:96
  443.8 12.6 %reshape.1690 = bf16[10240,2,6]{2,1,0:T(2,128)(2,1)} reshape(bf16[4,2,15360]{2,1,0:T(2,128)(2,1)S(1)} %all-to-all-done.4) | data formatting | bytes 491520
  456.4 10.2 %copy.680 = bf16[2,6,4,2560]{3,0,2,1:T(2,128)(2,1)S(1)} copy(bf16[2,6,4,2560]{1,0,3,2:T(2,128)(2,1)} %bitcast.1166) | data formatting | bytes 491520 | tf_op jit(solution)/shard_map/all_to_all | solution.py:95
  576.0 12.6 %reshape.1700 = bf16[10240,2,6]{2,1,0:T(2,128)(2,1)} reshape(bf16[4,2,15360]{2,1,0:T(2,128)(2,1)S(1)} %all-to-all-done.12) | data formatting | bytes 491520
  588.6 12.2 %copy.904 = bf16[2,6,4,2560]{3,2,0,1:T(4,128)(2,1)S(1)} copy(bf16[2,6,4,2560]{1,0,3,2:T(2,128)(2,1)} %bitcast.1168) | data formatting | bytes 491520 | tf_op jit(solution)/shard_map/all_to_all | solution.py:96
  602.2 12.6 %reshape.1692 = bf16[10240,2,6]{2,1,0:T(2,128)(2,1)} reshape(bf16[4,2,15360]{2,1,0:T(2,128)(2,1)S(1)} %all-to-all-done.6) | data formatting | bytes 491520
  614.8 10.2 %copy.708 = bf16[2,6,4,2560]{3,0,2,1:T(2,128)(2,1)S(1)} copy(bf16[2,6,4,2560]{1,0,3,2:T(2,128)(2,1)} %bitcast.1169) | data formatting | bytes 491520 | tf_op jit(solution)/shard_map/all_to_all | solution.py:95
  733.5 12.6 %reshape.1702 = bf16[10240,2,6]{2,1,0:T(2,128)(2,1)} reshape(bf16[4,2,15360]{2,1,0:T(2,128)(2,1)S(1)} %all-to-all-done.13) | data formatting | bytes 491520
  746.1 12.2 %copy.905 = bf16[2,6,4,2560]{3,2,0,1:T(4,128)(2,1)S(1)} copy(bf16[2,6,4,2560]{1,0,3,2:T(2,128)(2,1)} %bitcast.1171) | data formatting | bytes 491520 | tf_op jit(solution)/shard_map/all_to_all | solution.py:96
  759.7 12.6 %reshape.1694 = bf16[10240,2,6]{2,1,0:T(2,128)(2,1)} reshape(bf16[4,2,15360]{2,1,0:T(2,128)(2,1)S(1)} %all-to-all-done.8) | data formatting | bytes 491520
  772.3 10.2 %copy.736 = bf16[2,6,4,2560]{3,0,2,1:T(2,128)(2,1)S(1)} copy(bf16[2,6,4,2560]{1,0,3,2:T(2,128)(2,1)} %bitcast.1172) | data formatting | bytes 491520 | tf_op jit(solution)/shard_map/all_to_all | solution.py:95
  838.7 10.3 %copy.821 = bf16[2,6,10240]{1,0,2:T(2,128)(2,1)} copy(bf16[2,6,10240]{2,0,1:T(2,128)(2,1)} %get-tuple-element.3) | data formatting | bytes 491520 | tf_op jit(solution)/shard_map/convert_element_type | solution.py:92
  867.9 12.6 %reshape.1704 = bf16[10240,2,6]{2,1,0:T(2,128)(2,1)} reshape(bf16[4,2,15360]{2,1,0:T(2,128)(2,1)S(1)} %all-to-all-done.14) | data formatting | bytes 491520
  880.6 12.3 %copy.906 = bf16[2,6,4,2560]{3,2,0,1:T(4,128)(2,1)S(1)} copy(bf16[2,6,4,2560]{1,0,3,2:T(2,128)(2,1)} %bitcast.1174) | data formatting | bytes 491520 | tf_op jit(solution)/shard_map/all_to_all | solution.py:96
  894.5 23.7 %psum.15 = f32[1,3,64,64]{3,2,1,0:T(8,128)} all-reduce(f32[1,3,64,64]{3,2,1,0:T(8,128)S(1)} %fusion.170), channel_id=1, replica_groups=mesh['section'=4,'tm'=4,'batch'=2] {'tm','batch'}, use_global_device_ids=true, to_apply=%region_1.2 | all-reduce | flops 12288 | bytes 98304 | tf_op jit(solution)/shard_map/psum | solution.py:134
  (836 shorter events, 614.8 us)
Async XLA Ops:
  26.5 101.1 %all-to-all-start = ((bf16[4,2,15360]{2,1,0:T(2,128)(2,1)}), bf16[4,2,15360]{2,1,0:T(2,128)(2,1)}, u32[]{:S(2)}, u32[]{:S(2)}) async-start(bf16[4,2,15360]{2,1,0:T(2,128)(2,1)} %reshape.1685), calls=%async_computation | async-start | bytes 491520 | tf_op jit(solution)/shard_map/all_to_all | solution.py:95
  35.0 160.8 %copy-start.16 = (bf16[128,128,1,1]{1,0,2,3:T(8,128)(2,1)}, bf16[128,128,1,1]{1,0,2,3:T(8,128)(2,1)S(1)}, u32[]{:S(2)}) copy-start(bf16[128,128,1,1]{1,0,2,3:T(8,128)(2,1)S(1)} %reshape.1603) | copy-start | bytes 98308
  35.1 160.9 %copy-start.11 = (bf16[128,128,1,1]{1,0,2,3:T(8,128)(2,1)}, bf16[128,128,1,1]{1,0,2,3:T(8,128)(2,1)S(1)}, u32[]{:S(2)}) copy-start(bf16[128,128,1,1]{1,0,2,3:T(8,128)(2,1)S(1)} %reshape.1604) | copy-start | bytes 98308
  35.2 161.1 %copy-start.6 = (bf16[128,128,1,1]{1,0,2,3:T(8,128)(2,1)}, bf16[128,128,1,1]{1,0,2,3:T(8,128)(2,1)S(1)}, u32[]{:S(2)}) copy-start(bf16[128,128,1,1]{1,0,2,3:T(8,128)(2,1)S(1)} %reshape.1605) | copy-start | bytes 98308
  35.3 162.2 %copy-start.1 = (bf16[128,128,1,1]{1,0,2,3:T(8,128)(2,1)}, bf16[128,128,1,1]{1,0,2,3:T(8,128)(2,1)S(1)}, u32[]{:S(2)}) copy-start(bf16[128,128,1,1]{1,0,2,3:T(8,128)(2,1)S(1)} %reshape.1606) | copy-start | bytes 98308
  154.9 10.0 %all-to-all-start.1 = ((bf16[8,6,2560]{2,1,0:T(8,128)(2,1)}), bf16[8,6,2560]{2,1,0:T(8,128)(2,1)S(1)}, u32[]{:S(2)}, u32[]{:S(2)}) async-start(bf16[8,6,2560]{2,1,0:T(8,128)(2,1)} %reshape.1671), calls=%async_computation.1 | async-start | bytes 655360 | tf_op jit(solution)/shard_map/all_to_all | solution.py:100
  204.0 29.9 %collective-permute-start = (bf16[2,6,10240]{2,0,1:T(2,128)(2,1)S(1)}, bf16[2,6,10240]{2,0,1:T(2,128)(2,1)S(1)}, u32[]{:S(2)}, u32[]{:S(2)}) collective-permute-start(bf16[2,6,10240]{2,0,1:T(2,128)(2,1)S(1)} %add_convert_fusion.5), channel_id=1, source_target_pairs={{8,0},{16,8},{24,16},{9,1},{17,9},{25,17},{10,2},{18,10},{26,18},{... | collective-permute-start | bytes 737288 | tf_op jit(solution)/shard_map/ppermute | solution.py:12
  225.6 26.6 %all-to-all-start.10 = ((bf16[4,2,15360]{2,1,0:T(2,128)(2,1)}), bf16[4,2,15360]{2,1,0:T(2,128)(2,1)S(1)}, u32[]{:S(2)}, u32[]{:S(2)}) async-start(bf16[4,2,15360]{2,1,0:T(2,128)(2,1)} %reshape.1695), calls=%async_computation.10 | async-start | bytes 491520 | tf_op jit(solution)/shard_map/all_to_all | solution.py:96
  252.2 31.3 %all-to-all-start.2 = ((bf16[4,2,15360]{2,1,0:T(2,128)(2,1)}), bf16[4,2,15360]{2,1,0:T(2,128)(2,1)S(1)}, u32[]{:S(2)}, u32[]{:S(2)}) async-start(bf16[4,2,15360]{2,1,0:T(2,128)(2,1)} %reshape.1687), calls=%async_computation.2 | async-start | bytes 491520 | tf_op jit(solution)/shard_map/all_to_all | solution.py:95
  315.0 10.0 %all-to-all-start.3 = ((bf16[8,6,2560]{2,1,0:T(8,128)(2,1)}), bf16[8,6,2560]{2,1,0:T(8,128)(2,1)}, u32[]{:S(2)}, u32[]{:S(2)}) async-start(bf16[8,6,2560]{2,1,0:T(8,128)(2,1)} %reshape.1681), calls=%async_computation.3 | async-start | bytes 655360 | tf_op jit(solution)/shard_map/all_to_all | solution.py:100
  364.2 30.1 %collective-permute-start.1 = (bf16[2,6,10240]{2,0,1:T(2,128)(2,1)S(1)}, bf16[2,6,10240]{2,0,1:T(2,128)(2,1)S(1)}, u32[]{:S(2)}, u32[]{:S(2)}) collective-permute-start(bf16[2,6,10240]{2,0,1:T(2,128)(2,1)S(1)} %add_convert_fusion.4), channel_id=1, source_target_pairs={{8,0},{16,8},{24,16},{9,1},{17,9},{25,17},{10,2},{18,10},{26,18},{... | collective-permute-start | bytes 737288 | tf_op jit(solution)/shard_map/ppermute | solution.py:12
  385.8 26.9 %all-to-all-start.11 = ((bf16[4,2,15360]{2,1,0:T(2,128)(2,1)}), bf16[4,2,15360]{2,1,0:T(2,128)(2,1)S(1)}, u32[]{:S(2)}, u32[]{:S(2)}) async-start(bf16[4,2,15360]{2,1,0:T(2,128)(2,1)} %reshape.1697), calls=%async_computation.11 | async-start | bytes 491520 | tf_op jit(solution)/shard_map/all_to_all | solution.py:96
  412.7 31.1 %all-to-all-start.4 = ((bf16[4,2,15360]{2,1,0:T(2,128)(2,1)}), bf16[4,2,15360]{2,1,0:T(2,128)(2,1)S(1)}, u32[]{:S(2)}, u32[]{:S(2)}) async-start(bf16[4,2,15360]{2,1,0:T(2,128)(2,1)} %reshape.1689), calls=%async_computation.4 | async-start | bytes 491520 | tf_op jit(solution)/shard_map/all_to_all | solution.py:95
  475.3 10.0 %all-to-all-start.5 = ((bf16[8,6,2560]{2,1,0:T(8,128)(2,1)}), bf16[8,6,2560]{2,1,0:T(8,128)(2,1)}, u32[]{:S(2)}, u32[]{:S(2)}) async-start(bf16[8,6,2560]{2,1,0:T(8,128)(2,1)} %reshape.1682), calls=%async_computation.5 | async-start | bytes 655360 | tf_op jit(solution)/shard_map/all_to_all | solution.py:100
  522.6 30.0 %collective-permute-start.2 = (bf16[2,6,10240]{2,0,1:T(2,128)(2,1)S(1)}, bf16[2,6,10240]{2,0,1:T(2,128)(2,1)S(1)}, u32[]{:S(2)}, u32[]{:S(2)}) collective-permute-start(bf16[2,6,10240]{2,0,1:T(2,128)(2,1)S(1)} %add_convert_fusion.3), channel_id=1, source_target_pairs={{8,0},{16,8},{24,16},{9,1},{17,9},{25,17},{10,2},{18,10},{26,18},{... | collective-permute-start | bytes 737288 | tf_op jit(solution)/shard_map/ppermute | solution.py:12
  544.1 26.8 %all-to-all-start.12 = ((bf16[4,2,15360]{2,1,0:T(2,128)(2,1)}), bf16[4,2,15360]{2,1,0:T(2,128)(2,1)S(1)}, u32[]{:S(2)}, u32[]{:S(2)}) async-start(bf16[4,2,15360]{2,1,0:T(2,128)(2,1)} %reshape.1699), calls=%async_computation.12 | async-start | bytes 491520 | tf_op jit(solution)/shard_map/all_to_all | solution.py:96
  570.9 31.3 %all-to-all-start.6 = ((bf16[4,2,15360]{2,1,0:T(2,128)(2,1)}), bf16[4,2,15360]{2,1,0:T(2,128)(2,1)S(1)}, u32[]{:S(2)}, u32[]{:S(2)}) async-start(bf16[4,2,15360]{2,1,0:T(2,128)(2,1)} %reshape.1691), calls=%async_computation.6 | async-start | bytes 491520 | tf_op jit(solution)/shard_map/all_to_all | solution.py:95
  633.7 10.2 %all-to-all-start.7 = ((bf16[8,6,2560]{2,1,0:T(8,128)(2,1)}), bf16[8,6,2560]{2,1,0:T(8,128)(2,1)}, u32[]{:S(2)}, u32[]{:S(2)}) async-start(bf16[8,6,2560]{2,1,0:T(8,128)(2,1)} %reshape.1683), calls=%async_computation.7 | async-start | bytes 655360 | tf_op jit(solution)/shard_map/all_to_all | solution.py:100
  683.8 26.4 %collective-permute-start.3 = (bf16[2,6,10240]{2,0,1:T(2,128)(2,1)S(1)}, bf16[2,6,10240]{2,0,1:T(2,128)(2,1)S(1)}, u32[]{:S(2)}, u32[]{:S(2)}) collective-permute-start(bf16[2,6,10240]{2,0,1:T(2,128)(2,1)S(1)} %add_convert_fusion.2), channel_id=1, source_target_pairs={{8,0},{16,8},{24,16},{9,1},{17,9},{25,17},{10,2},{18,10},{26,18},{... | collective-permute-start | bytes 737288 | tf_op jit(solution)/shard_map/ppermute | solution.py:12
  705.3 23.3 %all-to-all-start.13 = ((bf16[4,2,15360]{2,1,0:T(2,128)(2,1)}), bf16[4,2,15360]{2,1,0:T(2,128)(2,1)S(1)}, u32[]{:S(2)}, u32[]{:S(2)}) async-start(bf16[4,2,15360]{2,1,0:T(2,128)(2,1)} %reshape.1701), calls=%async_computation.13 | async-start | bytes 491520 | tf_op jit(solution)/shard_map/all_to_all | solution.py:96
  728.6 31.1 %all-to-all-start.8 = ((bf16[4,2,15360]{2,1,0:T(2,128)(2,1)}), bf16[4,2,15360]{2,1,0:T(2,128)(2,1)S(1)}, u32[]{:S(2)}, u32[]{:S(2)}) async-start(bf16[4,2,15360]{2,1,0:T(2,128)(2,1)} %reshape.1693), calls=%async_computation.8 | async-start | bytes 491520 | tf_op jit(solution)/shard_map/all_to_all | solution.py:95
  786.3 9.9 %all-to-all-start.9 = ((bf16[8,6,2560]{2,1,0:T(8,128)(2,1)}), bf16[8,6,2560]{2,1,0:T(8,128)(2,1)S(1)}, u32[]{:S(2)}, u32[]{:S(2)}) async-start(bf16[8,6,2560]{2,1,0:T(8,128)(2,1)} %reshape.1684), calls=%async_computation.9 | async-start | bytes 655360 | tf_op jit(solution)/shard_map/all_to_all | solution.py:100
  790.6 127.5 %all-reduce.17.cloned.1.call-start = ((), (), s32[]{:S(2)}) async-start(), calls=%async_computation.15 | async-start | bytes 589824 | tf_op jit(solution)/shard_map/psum | solution.py:134
  858.9 9.0 all-to-all-start.14
  (175 other events, 2755.2 us)
Sparse Core Ops, SparseCore 0:
  818.2 57.1 all-reduce.16
where the time goes:
time: 944 us; the launch traced here: 927 us
  local copies, waits for them, and re-layouts  609 us (65%)
  matrix products  137 us (15%)
  starting transfers between devices  67.4 us (7%)
  other arithmetic  49 us (5%)
  blocking collectives  23.7 us (3%)
  waiting for transfers between devices  23.2 us (2%)
  between operations  17.9 us (2%)
    unnamed x379, local copies, waits for them, and re-layouts  229 us
    reshape x105, local copies, waits for them, and re-layouts, split_pixels(): return a.reshape(a.shape[:-1] + (a.shape[-1] // chans, chans))  112 us
    all_to_all x10, local copies, waits for them, and re-layouts, section_backward(): lax.all_to_all(h, 'tm', split_axis=2, concat_axis=0, tiled=True)  61.8 us
    dot_general x45, matrix products, spatial_back(): jnp.einsum('nrpa,nrpb->ab', xpiece, gz_pairs, preferred_element_type=jnp....  54.5 us
    all_to_all x10, local copies, waits for them, and re-layouts, section_backward(): lax.all_to_all(gradient_piece, 'tm', split_axis=2, concat_axis=0, tiled=T...  52.1 us
    convert_element_type x5, local copies, waits for them, and re-layouts, section_backward(): h = (z * sig).astype(jnp.bfloat16)  51.3 us
    select_n x5, local copies, waits for them, and re-layouts, body(): incoming = jnp.where(section_idx == number_sections - 1, top_grad, received)  40.8 us
    dot_general x45, matrix products, spatial_fwd(): jnp.einsum('nrpa,ab->nrpb', piece, paired_kernel(ws[3 * i + j]), preferre...  28.6 us
  transfers between devices with their start and end apart: 20, of which 6 were waited for; matrix products, arithmetic and copies ran while one was open for 48% of the time, Pallas kernels for 0%

commit v1 on v0

v1 whole, which is shorter than its diff:
```python
import functools

import jax
import jax.numpy as jnp
from jax import lax
from jax.experimental import pallas as pl
from jax.experimental.pallas import tpu as pltpu
from jax.sharding import PartitionSpec as P

DILATION = 2
ROWS = 8
LANES = 128
HALO = 3


def neighbours(x):
    none = jnp.zeros_like(x[:, :1])
    after = jnp.concatenate([x[:, 1:], none], axis=1)
    before = jnp.concatenate([none, x[:, :-1]], axis=1)
    lane = lax.broadcasted_iota(jnp.int32, x.shape, 3)
    return jnp.where(lane < LANES // 2, after, before)


def flat(x):
    return x.reshape(-1, x.shape[-1])


def mm(a, b, dims):
    return lax.dot_general(a, b, (dims, ((), ())), preferred_element_type=jnp.float32)


def kernel(tiles, frame_pairs, x_ref, w_ref, out_ref, gs, ds):
    sections, bins = x_ref.shape[:2]
    chans = w_ref.shape[-1]
    pairs = gs.shape[1]
    ext = pairs * ROWS
    share = x_ref.shape[2] - ext
    piece = out_ref.shape[2] - tiles * ROWS - (tiles * ROWS) % 16
    tile_rows = out_ref.shape[2] - piece
    out_pairs = tile_rows // ROWS
    first = lax.axis_index("tm") * tiles - HALO
    shape = (bins, pairs, ROWS, LANES)
    place = first + lax.broadcasted_iota(jnp.int32, shape, 1)
    row = lax.broadcasted_iota(jnp.int32, shape, 2)
    inside = (place >= 0) & (place < frame_pairs) & (row < 6)
    zero = jnp.zeros((chans, chans), jnp.bfloat16)
    blank = jnp.zeros((1, pairs, ROWS, LANES), jnp.float32)
    centre = slice(HALO, HALO + tiles)

    wide = [
        jnp.concatenate([x_ref[s, n, ext:, :] for s in range(sections)], axis=0)
        for n in range(bins)
    ]
    g = jnp.stack([v[:ext].astype(jnp.float32).reshape(pairs, ROWS, LANES) for v in wide])
    for s in range(sections - 1, -1, -1):
        w = [w_ref[s, t] for t in range(12)]
        x = x_ref[s, :, 0:ext, :].astype(jnp.float32).reshape(shape)
        xx = jnp.concatenate([x, neighbours(x)], axis=3).astype(jnp.bfloat16)
        fwd = jnp.concatenate(
            [
                jnp.concatenate(
                    [
                        jnp.concatenate([w[3 * i + 1], w[3 * i]], axis=1),
                        jnp.concatenate([w[3 * i + 2], w[3 * i + 1]], axis=1),
                        jnp.concatenate([zero, w[3 * i + 2]], axis=1),
                        jnp.concatenate([w[3 * i], zero], axis=1),
                    ],
                    axis=0,
                )
                for i in range(3)
            ],
            axis=1,
        )
        back = jnp.concatenate(
            [
                jnp.concatenate(
                    [
                        jnp.concatenate([w[3 * i + 1], w[3 * i], zero, w[3 * i + 2]], axis=1),
                        jnp.concatenate([w[3 * i + 2], w[3 * i + 1], w[3 * i], zero], axis=1),
                    ],
                    axis=0,
                )
                for i in range(3)
            ],
            axis=1,
        )
        time = jnp.concatenate(
            [
                jnp.concatenate([w[9], zero, w[10], zero, w[11], zero], axis=1),
                jnp.concatenate([zero, w[9], zero, w[10], zero, w[11]], axis=1),
            ],
            axis=0,
        )
        y = mm(flat(xx), fwd, ((1,), (0,)))
        part = [y[:, LANES * i : LANES * (i + 1)].reshape(-1, ROWS, LANES) for i in range(3)]
        z = part[1] + pltpu.roll(part[0], 1, 1) + pltpu.roll(part[2], ROWS - 1, 1)
        z = z.reshape(shape)
        sig = jax.nn.sigmoid(z)
        h = (z * sig).astype(jnp.bfloat16)
        slope = sig * (1.0 + z * (1.0 - sig))
        after = jnp.concatenate([g[1:], blank], axis=0)
        before = jnp.concatenate([blank, g[:-1]], axis=0)
        g3 = jnp.concatenate([after, g, before], axis=3).astype(jnp.bfloat16)
        gh = mm(flat(g3), time, ((1,), (1,))).astype(jnp.bfloat16)
        gz = (gh.astype(jnp.float32).reshape(shape) * slope).astype(jnp.bfloat16)
        gz = gz.astype(jnp.float32)
        flat_gz = gz.reshape(-1, ROWS, LANES)
        gg = [
            pltpu.roll(flat_gz, ROWS - 1, 1).reshape(shape),
            gz,
            pltpu.roll(flat_gz, 1, 1).reshape(shape),
        ]
        sides = []
        for v in gg:
            sides += [v, neighbours(v)]
        gsides = jnp.concatenate(sides, axis=3).astype(jnp.bfloat16)
        gs_in = mm(flat(gsides), back, ((1,), (1,))).reshape(shape)
        result = jnp.where(inside, g + gs_in, 0.0).astype(jnp.bfloat16)
        old = g
        g = result.astype(jnp.float32)
        out_ref[s, :, 0:tile_rows, :] = (
            g[:, HALO : HALO + out_pairs].reshape(bins, tile_rows, LANES).astype(jnp.bfloat16)
        )
        g3c = g3.astype(jnp.float32)[:, centre].astype(jnp.bfloat16)
        hc = h.astype(jnp.float32)[:, centre].astype(jnp.bfloat16)
        xc = xx.astype(jnp.float32)[:, centre].astype(jnp.bfloat16)
        gc = jnp.concatenate([v[:, centre] for v in gg], axis=3).astype(jnp.bfloat16)
        dt = mm(flat(hc), flat(g3c), ((0,), (0,)))
        d = mm(flat(xc), flat(gc), ((0,), (0,)))

        def block(a, r, i, b):
            at = i * LANES + b * chans
            return a[r * chans : (r + 1) * chans, at : at + chans]

        taps = []
        for i in range(3):
            taps.append(block(d, 0, i, 1) + block(d, 3, i, 0))
            taps.append(block(d, 0, i, 0) + block(d, 1, i, 1))
            taps.append(block(d, 1, i, 0) + block(d, 2, i, 1))
        for k in range(3):
            taps.append(block(dt, 0, k, 0) + block(dt, 1, k, 1))
        for k in range(6):
            ds[k * chans : (k + 1) * chans, :] = jnp.concatenate(
                [taps[2 * k], taps[2 * k + 1]], axis=1
            )
        for n in range(bins):
            got = piece * n
            rows = 6 * chans // bins
            out_ref[s, n, tile_rows : tile_rows + rows, :] = ds[
                rows * n : rows * (n + 1), :
            ].astype(jnp.bfloat16)


def pack(a, tm, tiles, pairs):
    micro, local, rows, width = a.shape
    frame = width // LANES
    a = jnp.pad(a, ((0, 0), (0, 0), (0, ROWS - rows), (0, 0)))
    a = a.reshape(micro * local, ROWS, frame, LANES).transpose(0, 2, 1, 3)
    a = jnp.pad(a, ((0, 0), (HALO, pairs), (0, 0), (0, 0)))
    cut = [a[:, tiles * m : tiles * m + pairs] for m in range(tm)]
    return jnp.stack(cut, axis=1).reshape(micro * local * tm, pairs * ROWS, LANES)


def body(acts, cot, spatial_weight, temporal_weight):
    sections, tm = lax.axis_size("section"), lax.axis_size("tm")
    both = ("section", "tm")
    micro, local, rows, width = cot.shape
    chans = spatial_weight.shape[-1]
    frame = width // LANES
    tiles = frame // tm
    pairs = tiles + 2 * HALO
    pairs += pairs % 2
    ext = pairs * ROWS
    share = -(-ext // (16 * sections)) * 16
    weights = lax.all_gather(
        jnp.concatenate([spatial_weight[0], temporal_weight[0]]), "section", axis=0
    )
    mine = pack(acts[0], tm, tiles, pairs)
    top = pack(cot, tm, tiles, pairs)
    top = jnp.pad(top, ((0, 0), (0, share * sections - ext), (0, 0)))
    top = lax.dynamic_slice_in_dim(top, lax.axis_index("section") * share, share, 1)
    message = jnp.concatenate([mine, top], axis=1)
    got = lax.all_to_all(message, both, 0, 0, tiled=True)
    got = got.reshape(sections, tm, ext + share, LANES)
    tile_rows = tiles * ROWS + (tiles * ROWS) % 16
    piece = 6 * chans // tm
    out = pl.pallas_call(
        functools.partial(kernel, tiles, frame),
        out_shape=jax.ShapeDtypeStruct((sections, tm, tile_rows + piece, LANES), jnp.bfloat16),
        in_specs=[pl.BlockSpec(memory_space=pltpu.VMEM)] * 2,
        out_specs=pl.BlockSpec(memory_space=pltpu.VMEM),
        scratch_shapes=[
            pltpu.VMEM((1, pairs, ROWS, LANES), jnp.float32),
            pltpu.VMEM((6 * chans, LANES), jnp.float32),
        ],
        compiler_params=pltpu.CompilerParams(vmem_limit_bytes=48 * 2**20),
    )(got, weights)
    home = lax.all_to_all(
        out.reshape(sections * tm, tile_rows + piece, LANES), both, 0, 0, tiled=True
    )
    grad = home[:, : tiles * ROWS].reshape(micro, local, tm * tiles, ROWS, LANES)
    grad = grad.transpose(0, 1, 3, 2, 4)[:, :, :rows].reshape(micro, local, rows, width)
    partial = jnp.sum(home[:, tile_rows:].astype(jnp.float32), axis=0)
    full = jnp.sum(lax.all_gather(partial, ("tm", "batch"), axis=0).reshape(tm, -1, piece, LANES), axis=1)
    full = full.reshape(6, chans, 2, chans).transpose(0, 2, 1, 3).reshape(12, chans, chans)
    return grad[None], full[None, :9], full[None, 9:]


def solution(mesh):
    in_specs = (
        P("section", "batch", "tm", None, None),
        P("batch", "tm", None, None),
        P("section", None, None, None),
        P("section", None, None, None),
    )
    out_specs = (
        P("section", "batch", "tm", None, None),
        P("section", None, None, None),
        P("section", None, None, None),
    )
    return jax.shard_map(body, mesh=mesh, in_specs=in_specs, out_specs=out_specs, check_vma=False)
```

time: 944 us -> 100 us (0.11); the launches traced: 927 us -> 99.9 us
  local copies, waits for them, and re-layouts: 609 us -> 6.73 us
  matrix products: 137 us -> 0 us
  starting transfers between devices: 67.4 us -> 8.44 us
  blocking collectives: 23.7 us -> 77.9 us
  other arithmetic: 49 us -> 1.53 us
  waiting for transfers between devices: 23.2 us -> 0.01 us
  between operations: 17.9 us -> 0.81 us
    unnamed x379 -> x10, local copies, waits for them, and re-layouts: 229 us -> 2.17 us
    dot_general x165 -> x0, matrix products: 137 us -> none  [the longest x45 54.5 us: spatial_back(): jnp.einsum('nrpa,nrpb->ab', xpiece, gz_pairs, preferred_element_type=jnp....]
    all_to_all x20 -> x0, local copies, waits for them, and re-layouts: 114 us -> none  [the longest x10 61.8 us: section_backward(): lax.all_to_all(h, 'tm', split_axis=2, concat_axis=0, tiled=True)]
    reshape x105 -> x2, local copies, waits for them, and re-layouts: 112 us -> 0.33 us  [the longest x1 0.24 us: body(): full.reshape(6, chans, 2, chans).transpose(0, 2, 1, 3)]
    convert_element_type x26 -> x0, local copies, waits for them, and re-layouts: 67.9 us -> none  [the longest x5 51.3 us: section_backward(): h = (z * sig).astype(jnp.bfloat16)]
    all_to_all x15 -> x1, starting transfers between devices: 62.1 us -> 8.44 us  [body(): got = lax.all_to_all(message, both, 0, 0, tiled=True)]
    all_gather x0 -> x2, blocking collectives: none -> 49.5 us  [the longest x1 40.5 us: body(): lax.all_gather(jnp.concatenate([spatial_weight[0], temporal_weight[0]]),...]
    select_n x5 -> x0, local copies, waits for them, and re-layouts: 40.8 us -> none  [body(): incoming = jnp.where(section_idx == number_sections - 1, top_grad, received)]
  transfers between devices with their start and end apart: 20 -> 1, of which waited for: 6 -> 0; matrix products, arithmetic and copies ran while one was open for 48% -> 0% of each run, Pallas kernels for 0% -> 0%
where the time goes in v1:
time: 100 us; the launch traced here: 99.9 us
  blocking collectives  77.9 us (78%)
  starting transfers between devices  8.44 us (8%)
  local copies, waits for them, and re-layouts  6.73 us (7%)
  Pallas kernels  4.54 us (5%)
  other arithmetic  1.53 us (2%)
    all_gather x1, blocking collectives, body(): lax.all_gather(jnp.concatenate([spatial_weight[0], temporal_weight[0]]),...  40.5 us
    all_to_all x1, blocking collectives, body(): lax.all_to_all(out.reshape(sections * tm, tile_rows + piece, LANES), both...  28.3 us
    all_gather x1, blocking collectives, body(): lax.all_gather(partial, ('tm', 'batch'), axis=0)  8.99 us
    all_to_all x1, starting transfers between devices, body(): got = lax.all_to_all(message, both, 0, 0, tiled=True)  8.44 us
    pallas_call x1, Pallas kernels, body(): pl.pallas_call(functools.partial(kernel, tiles, frame), out_shape=jax.Sha...  4.54 us
    unnamed x10, local copies, waits for them, and re-layouts  2.17 us
  transfers between devices with their start and end apart: 1, of which 0 were waited for; matrix products, arithmetic and copies ran while one was open for 0% of the time, Pallas kernels for 0%

profile of v1, /device:TPU:0, one launch (start us, length us, event | category | flops | bytes accessed | tf_op | source)
XLA Modules:
  0.0 99.9 jit_solution(15378435838425030421)
XLA Ops:
  0.6 1.2 %copy.36 = bf16[2,2,6,10240]{3,2,1,0:T(8,128)(2,1)S(1)} copy(bf16[2,2,6,10240]{3,1,2,0:T(2,128)(2,1)} %param.5) | data formatting | bytes 983040
  1.8 0.1 pad.20.clone
  1.9 0.1 copy.42
  2.0 0.4 fusion.2
  2.5 0.2 pad_maximum_fusion.2
  2.6 0.4 copy.32
  3.0 0.6 copy-done
  3.7 0.2 copy.35
  3.8 0.1 pad.18.clone
  3.9 0.1 copy.43
  4.0 0.4 fusion
  4.5 0.2 pad_maximum_fusion.1
  4.6 0.4 copy.30
  5.1 1.1 %pad_maximum_fusion = bf16[16,272,128]{2,1,0:T(8,128)(2,1)} fusion(bf16[16,64,128]{2,1,0:T(8,128)(2,1)S(1)} %pad_dynamic-slice_fusion, bf16[16,208,128]{2,1,0:T(8,128)(2,1)S(1)} %bitcast.64), kind=kLoop, calls=%fused_computation | loop fusion | flops 2228224 | bytes 2228224 | tf_op jit(solution)/shard_map/concatenate | solution.py:182
  6.2 8.4 %all-to-all-start = ((bf16[16,272,128]{2,1,0:T(8,128)(2,1)}), bf16[16,272,128]{2,1,0:T(8,128)(2,1)S(1)}, u32[]{:S(2)}, u32[]{:S(2)}) async-start(bf16[16,272,128]{2,1,0:T(8,128)(2,1)} %pad_maximum_fusion), calls=%async_computation | async-start | bytes 2228224 | tf_op jit(solution)/shard_map/all_to_all | solution.py:183
  14.7 40.5 %all-gather = bf16[48,64,64]{2,1,0:T(8,128)(2,1)S(1)} all-gather(bf16[12,64,64]{2,1,0:T(8,128)(2,1)S(1)} %pad_maximum_fusion.3), channel_id=2, replica_groups=mesh['section'=4,'tm'=4,'batch'=2] {'section'}, dimensions={0}, use_global_device_ids=true | all-gather | bytes 491520 | tf_op jit(solution)/shard_map/all_gather | solution.py:175
  55.2 4.5 %shard_map.67 = bf16[4,4,256,128]{3,2,1,0:T(8,128)(2,1)S(1)} custom-call(bf16[4,4,272,128]{3,2,1,0:T(8,128)(2,1)S(1)} %bitcast.59, bf16[4,12,64,64]{3,2,1,0:T(8,128)(2,1)S(1)} %bitcast.61), custom_call_target="tpu_custom_call" | custom-call | tf_op jit(solution)/shard_map/pallas_call | solution.py:187
  59.8 28.3 %all_to_all.10 = bf16[16,256,128]{2,1,0:T(8,128)(2,1)S(1)} all-to-all(bf16[16,256,128]{2,1,0:T(8,128)(2,1)S(1)} %bitcast.60), channel_id=1, replica_groups=mesh['section'=4,'tm'=4,'batch'=2] {'section','tm'}, dimensions={0} | all-to-all | bytes 2097152 | tf_op jit(solution)/shard_map/all_to_all | solution.py:198
  88.2 9.0 %all-gather.1 = f32[768,128]{1,0:T(8,128)S(1)} all-gather(f32[96,128]{1,0:T(8,128)S(1)} %convert_reduce_fusion), channel_id=3, replica_groups=mesh['section'=4,'tm'=4,'batch'=2] {'tm','batch'}, dimensions={0}, use_global_device_ids=true | all-gather | bytes 442368 | tf_op jit(solution)/shard_map/all_gather | solution.py:204
  97.2 0.2 reshape.44
  97.5 0.7 slice_bitcast_fusion
  98.2 0.6 slice_bitcast_fusion.5
  98.9 0.1 copy.44
  99.0 0.9 broadcast_in_dim_reshape.3
  (13 shorter events, 0.3 us)
Async XLA Ops:
  2.6 1.0 %copy-start = (bf16[1,2,2,6,10240]{4,2,3,1,0:T(2,128)(2,1)S(1)}, bf16[1,2,2,6,10240]{4,2,3,1,0:T(2,128)(2,1)}, u32[]{:S(2)}) copy-start(bf16[1,2,2,6,10240]{4,2,3,1,0:T(2,128)(2,1)} %param.4) | copy-start | bytes 1474564
  6.1 8.5 %copy-start.1 = (bf16[1,9,64,64]{3,2,1,0:T(8,128)(2,1)S(1)}, bf16[1,9,64,64]{3,2,1,0:T(8,128)(2,1)}, u32[]{:S(2)}) copy-start(bf16[1,9,64,64]{3,2,1,0:T(8,128)(2,1)} %param.6) | copy-start | bytes 221188
  6.2 8.5 %copy-start.2 = (bf16[1,3,64,64]{3,2,1,0:T(8,128)(2,1)S(1)}, bf16[1,3,64,64]{3,2,1,0:T(8,128)(2,1)}, u32[]{:S(2)}) copy-start(bf16[1,3,64,64]{3,2,1,0:T(8,128)(2,1)} %param.7) | copy-start | bytes 73732
  6.2 49.0 %all-to-all-start = ((bf16[16,272,128]{2,1,0:T(8,128)(2,1)}), bf16[16,272,128]{2,1,0:T(8,128)(2,1)S(1)}, u32[]{:S(2)}, u32[]{:S(2)}) async-start(bf16[16,272,128]{2,1,0:T(8,128)(2,1)} %pad_maximum_fusion), calls=%async_computation | async-start | bytes 2228224 | tf_op jit(solution)/shard_map/all_to_all | solution.py:183

commit v2 on v1

v2 whole, which is shorter than its diff:
```python
import functools

import jax
import jax.numpy as jnp
from jax import lax
from jax.experimental import pallas as pl
from jax.experimental.pallas import tpu as pltpu
from jax.sharding import PartitionSpec as P

DILATION = 2
ROWS = 8
LANES = 128
HALO = 3
MESH = pl.DeviceIdType.MESH


def neighbours(x):
    none = jnp.zeros_like(x[:, :1])
    after = jnp.concatenate([x[:, 1:], none], axis=1)
    before = jnp.concatenate([none, x[:, :-1]], axis=1)
    lane = lax.broadcasted_iota(jnp.int32, x.shape, 3)
    return jnp.where(lane < LANES // 2, after, before)


def flat(x):
    return x.reshape(-1, x.shape[-1])


def mm(a, b, dims):
    return lax.dot_general(a, b, (dims, ((), ())), preferred_element_type=jnp.float32)


def taps_of(d, dt, chans):
    def block(a, r, i, b):
        at = i * LANES + b * chans
        return a[r * chans : (r + 1) * chans, at : at + chans]

    taps = []
    for i in range(3):
        taps.append(block(d, 0, i, 1) + block(d, 3, i, 0))
        taps.append(block(d, 0, i, 0) + block(d, 1, i, 1))
        taps.append(block(d, 1, i, 0) + block(d, 2, i, 1))
    for k in range(3):
        taps.append(block(dt, 0, k, 0) + block(dt, 1, k, 1))
    return taps


def set_weights(ws_ref, wt_ref, fwd, back, time):
    chans = ws_ref.shape[-1]
    zero = jnp.zeros((chans, chans), jnp.bfloat16)
    for i in range(3):
        a, b, c = [ws_ref[3 * i + j] for j in range(3)]
        at = slice(i * LANES, (i + 1) * LANES)
        rows = [[b, a], [c, b], [zero, c], [a, zero]]
        fwd[:, at] = jnp.concatenate([jnp.concatenate(v, axis=1) for v in rows], axis=0)
        at = slice(i * 2 * LANES, (i + 1) * 2 * LANES)
        rows = [[b, a, zero, c], [c, b, a, zero]]
        back[:, at] = jnp.concatenate([jnp.concatenate(v, axis=1) for v in rows], axis=0)
        at = slice(i * LANES, (i + 1) * LANES)
        rows = [[wt_ref[i], zero], [zero, wt_ref[i]]]
        time[:, at] = jnp.concatenate([jnp.concatenate(v, axis=1) for v in rows], axis=0)


def pack(frame, stage, c, tiles):
    tm, pairs = stage.shape[0], stage.shape[2] // ROWS
    rows, width = frame.shape
    v = frame.astype(jnp.float32)
    v = jnp.concatenate([v, jnp.zeros((ROWS - rows, width), jnp.float32)], axis=0)
    zero = jnp.zeros((1, ROWS, LANES), jnp.float32)
    cut = [v[:, LANES * p : LANES * (p + 1)][None] for p in range(width // LANES)]
    cut = [zero] * HALO + cut + [zero] * pairs
    for m in range(tm):
        part = jnp.concatenate(cut[tiles * m : tiles * m + pairs], axis=0)
        stage[m, c] = part.reshape(pairs * ROWS, LANES).astype(jnp.bfloat16)


def kernel(
    sections, batches, tiles, acts, cot, ws_ref, wt_ref, out, grads,
    x_stage, g_stage, x_buf, g_buf, r_buf, o_buf, home, fwd, back, time, acc, acc_t, ds,
    w_send, w_recv, w_piece, w_full,
    x_sem, g_sem, z_sem, o_sem, w_sem, f_sem,
):
    tm = x_stage.shape[0]
    chains, frame_rows, width = acts.shape
    chans = ws_ref.shape[-1]
    ext = x_buf.shape[2]
    pairs = ext // ROWS
    tile_rows = o_buf.shape[2]
    out_pairs = tile_rows // ROWS
    group = tm * batches
    section, me, core = [lax.axis_index(a) for a in ("section", "tm", "batch")]
    rank = me * batches + core

    def member(e):
        other = lax.rem(rank + e, group)
        return other, (section, other // batches, lax.rem(other, batches))

    def peer(d):
        other = lax.rem(me + d, tm)
        return other, (section, other, core)

    barrier = pltpu.get_barrier_semaphore()
    for e in range(1, group):
        pl.semaphore_signal(barrier, inc=1, device_id=member(e)[1], device_id_type=MESH)

    @pl.when(section > 0)
    def _():
        pl.semaphore_signal(barrier, inc=1, device_id=(section - 1, me, core), device_id_type=MESH)

    @pl.when(section < sections - 1)
    def _():
        pl.semaphore_signal(barrier, inc=1, device_id=(section + 1, me, core), device_id_type=MESH)

    def copy(src, dst, sems, at, device):
        return pltpu.make_async_remote_copy(
            src_ref=src, dst_ref=dst, send_sem=sems.at[(0,) + at], recv_sem=sems.at[(1,) + at],
            device_id=device, device_id_type=MESH,
        )

    def x_copy(c, d):
        other, device = peer(d)
        return copy(x_stage.at[other, c], x_buf.at[c, me], x_sem, (c, d - 1), device)

    def g_copy(c, d):
        other, device = peer(d)
        return copy(g_stage.at[other, c], g_buf.at[c, me], g_sem, (c, d - 1), device)

    def z_copy(c):
        return copy(r_buf.at[c], g_buf.at[c], z_sem, (c,), (lax.max(section - 1, 0), me, core))

    def o_copy(c, d):
        other, device = peer(d)
        return copy(o_buf.at[c, other], home.at[c, me], o_sem, (c, d - 1), device)

    def w_copy(e):
        other, device = member(e)
        return copy(w_send.at[other], w_recv.at[rank], w_sem, (e - 1,), device)

    def f_copy(e):
        return copy(w_piece, w_full.at[rank], f_sem, (e - 1,), member(e)[1])

    pack(acts[0], x_stage, 0, tiles)

    @pl.when(section == sections - 1)
    def _():
        pack(cot[0], g_stage, 0, tiles)

    more = (section > 0).astype(jnp.int32) + (section < sections - 1).astype(jnp.int32)
    pl.semaphore_wait(barrier, group - 1 + more)

    def send(c, carry):
        @pl.when(c > 0)
        def _():
            pack(acts[c], x_stage, c, tiles)

            @pl.when(section == sections - 1)
            def _():
                pack(cot[c], g_stage, c, tiles)

        for d in range(1, tm):
            x_copy(c, d).start()
        x_buf[c, me] = x_stage[me, c]

        @pl.when(section == sections - 1)
        def _():
            for d in range(1, tm):
                g_copy(c, d).start()
            g_buf[c, me] = g_stage[me, c]

        return carry

    lax.fori_loop(0, chains, send, 0)
    set_weights(ws_ref, wt_ref, fwd, back, time)
    acc[...] = jnp.zeros_like(acc)
    acc_t[...] = jnp.zeros_like(acc_t)

    shape = (tm, pairs, ROWS, LANES)
    blank = jnp.zeros((1, pairs, ROWS, LANES), jnp.float32)
    centre = slice(HALO, HALO + tiles)

    def turn(c, carry):
        for d in range(1, tm):
            x_copy(c, d).wait_recv()
        x = x_buf[c].astype(jnp.float32).reshape(shape)
        xx = jnp.concatenate([x, neighbours(x)], axis=3)
        y = mm(flat(xx).astype(jnp.bfloat16), fwd[...], ((1,), (0,)))
        part = [y[:, LANES * i : LANES * (i + 1)].reshape(-1, ROWS, LANES) for i in range(3)]
        z = part[1] + pltpu.roll(part[0], 1, 1) + pltpu.roll(part[2], ROWS - 1, 1)
        z = z.reshape(shape)
        sig = jax.nn.sigmoid(z)
        h = z * sig
        slope = sig * (1.0 + z * (1.0 - sig))

        @pl.when(section == sections - 1)
        def _():
            for d in range(1, tm):
                g_copy(c, d).wait_recv()

        @pl.when(section < sections - 1)
        def _():
            z_copy(c).wait_recv()

        g = g_buf[c].astype(jnp.float32).reshape(shape)
        g3 = jnp.concatenate(
            [
                jnp.concatenate([g[1:], blank], axis=0),
                g,
                jnp.concatenate([blank, g[:-1]], axis=0),
            ],
            axis=3,
        )
        gh = mm(flat(g3).astype(jnp.bfloat16), time[...], ((1,), (1,))).astype(jnp.bfloat16)
        gz = (gh.astype(jnp.float32).reshape(shape) * slope).astype(jnp.bfloat16)
        gz = gz.astype(jnp.float32)
        flat_gz = gz.reshape(-1, ROWS, LANES)
        gg = [
            pltpu.roll(flat_gz, ROWS - 1, 1).reshape(shape),
            gz,
            pltpu.roll(flat_gz, 1, 1).reshape(shape),
        ]
        sides = []
        for v in gg:
            sides += [v, neighbours(v)]
        sides = jnp.concatenate(sides, axis=3).astype(jnp.bfloat16)
        inner = mm(flat(sides), back[...], ((1,), (1,))).reshape(shape)
        place = me * tiles - HALO + lax.broadcasted_iota(jnp.int32, shape, 1)
        row = lax.broadcasted_iota(jnp.int32, shape, 2)
        inside = (place >= 0) & (place < width // LANES) & (row < frame_rows)
        result = jnp.where(inside, g + inner, 0.0)
        r_buf[c] = result.reshape(tm, ext, LANES).astype(jnp.bfloat16)

        @pl.when(section > 0)
        def _():
            z_copy(c).start()

        o_buf[c] = (
            result[:, HALO : HALO + out_pairs].reshape(tm, tile_rows, LANES).astype(jnp.bfloat16)
        )
        for d in range(1, tm):
            o_copy(c, d).start()
        home[c, me] = o_buf[c, me]
        hc = flat(h[:, centre]).astype(jnp.bfloat16)
        acc_t[...] += mm(hc, flat(g3[:, centre]).astype(jnp.bfloat16), ((0,), (0,)))
        gc = jnp.concatenate([v[:, centre] for v in gg], axis=3).astype(jnp.bfloat16)
        acc[...] += mm(flat(xx[:, centre]).astype(jnp.bfloat16), flat(gc), ((0,), (0,)))
        return carry

    lax.fori_loop(0, chains, turn, 0)

    taps = taps_of(acc[...], acc_t[...], chans)
    for k in range(6):
        ds[k * chans : (k + 1) * chans, :] = jnp.concatenate([taps[2 * k], taps[2 * k + 1]], axis=1)
    rows = w_send.shape[1]
    for k in range(group):
        w_send[k] = ds[k * rows : (k + 1) * rows, :].astype(jnp.bfloat16)
    for e in range(1, group):
        w_copy(e).start()
    w_recv[rank] = w_send[rank]

    def unpack(c, carry):
        for d in range(1, tm):
            o_copy(c, d).wait_recv()
        v = home[c].astype(jnp.float32).reshape(tm, out_pairs, ROWS, LANES)
        cut = [v[m, p] for m in range(tm) for p in range(tiles)]
        out[c] = jnp.concatenate(cut, axis=1)[:frame_rows].astype(jnp.bfloat16)
        return carry

    lax.fori_loop(0, chains - 1, unpack, 0)
    for e in range(1, group):
        w_copy(e).wait_recv()
    w_piece[...] = jnp.sum(w_recv[...].astype(jnp.float32), axis=0)
    for e in range(1, group):
        f_copy(e).start()
    w_full[rank] = w_piece[...]
    unpack(chains - 1, 0)

    for e in range(1, group):
        f_copy(e).wait_recv()
    for k in range(group):
        ds[k * rows : (k + 1) * rows, :] = w_full[k]
    for t in range(12):
        both = ds[(t // 2) * chans : (t // 2 + 1) * chans, :]
        grads[t] = both[:, (t % 2) * chans : (t % 2 + 1) * chans]

    def finish(c, carry):
        for d in range(1, tm):
            x_copy(c, d).wait_send()
            o_copy(c, d).wait_send()

        @pl.when(section == sections - 1)
        def _():
            for d in range(1, tm):
                g_copy(c, d).wait_send()

        @pl.when(section > 0)
        def _():
            z_copy(c).wait_send()

        return carry

    lax.fori_loop(0, chains, finish, 0)
    for e in range(1, group):
        w_copy(e).wait_send()
        f_copy(e).wait_send()


def body(acts, cot, spatial_weight, temporal_weight):
    sections, tm, batches = [lax.axis_size(a) for a in ("section", "tm", "batch")]
    micro, local, rows, width = cot.shape
    chans = spatial_weight.shape[-1]
    chains = micro * local
    group = tm * batches
    tiles = width // LANES // tm
    pairs = tiles + 2 * HALO
    pairs += pairs % 2
    ext = pairs * ROWS
    tile_rows = tiles * ROWS + (tiles * ROWS) % 16
    piece = 6 * chans // group
    bf16, f32 = jnp.bfloat16, jnp.float32
    vmem, dma = pltpu.VMEM, pltpu.SemaphoreType.DMA
    grad, kernels = pl.pallas_call(
        functools.partial(kernel, sections, batches, tiles),
        out_shape=[
            jax.ShapeDtypeStruct((chains, rows, width), bf16),
            jax.ShapeDtypeStruct((12, chans, chans), f32),
        ],
        in_specs=[pl.BlockSpec(memory_space=vmem)] * 4,
        out_specs=[pl.BlockSpec(memory_space=vmem)] * 2,
        scratch_shapes=[
            vmem((tm, chains, ext, LANES), bf16),
            vmem((tm, chains, ext, LANES), bf16),
            vmem((chains, tm, ext, LANES), bf16),
            vmem((chains, tm, ext, LANES), bf16),
            vmem((chains, tm, ext, LANES), bf16),
            vmem((chains, tm, tile_rows, LANES), bf16),
            vmem((chains, tm, tile_rows, LANES), bf16),
            vmem((2 * LANES, 3 * LANES), bf16),
            vmem((LANES, 6 * LANES), bf16),
            vmem((LANES, 3 * LANES), bf16),
            vmem((2 * LANES, 3 * LANES), f32),
            vmem((LANES, 3 * LANES), f32),
            vmem((6 * chans, LANES), f32),
            vmem((group, piece, LANES), bf16),
            vmem((group, piece, LANES), bf16),
            vmem((piece, LANES), f32),
            vmem((group, piece, LANES), f32),
            dma((2, chains, tm - 1)),
            dma((2, chains, tm - 1)),
            dma((2, chains)),
            dma((2, chains, tm - 1)),
            dma((2, group - 1)),
            dma((2, group - 1)),
        ],
        compiler_params=pltpu.CompilerParams(
            collective_id=0, has_side_effects=True, vmem_limit_bytes=56 * 2**20
        ),
    )(acts.reshape(chains, rows, width), cot.reshape(chains, rows, width), spatial_weight[0], temporal_weight[0])
    return grad.reshape(acts.shape), kernels[None, :9], kernels[None, 9:]


def solution(mesh):
    in_specs = (
        P("section", "batch", "tm", None, None),
        P("batch", "tm", None, None),
        P("section", None, None, None),
        P("section", None, None, None),
    )
    out_specs = (
        P("section", "batch", "tm", None, None),
        P("section", None, None, None),
        P("section", None, None, None),
    )
    return jax.shard_map(body, mesh=mesh, in_specs=in_specs, out_specs=out_specs, check_vma=False)
```

time: 100 us -> 65.6 us (0.66)
  blocking collectives: 77.9 us -> 0 us
  Pallas kernels: 4.54 us -> 57.9 us
  starting transfers between devices: 8.44 us -> 0 us
  other arithmetic: 1.53 us -> 0 us
    pallas_call x1, Pallas kernels: 4.54 us -> 57.9 us  [body(): pl.pallas_call(functools.partial(kernel, sections, batches, tiles), out_s...]
    all_gather x2 -> x0, blocking collectives: 49.5 us -> none  [the longest x1 40.5 us: body(): lax.all_gather(jnp.concatenate([spatial_weight[0], temporal_weight[0]]),...]
    all_to_all x1 -> x0, blocking collectives: 28.3 us -> none  [body(): lax.all_to_all(out.reshape(sections * tm, tile_rows + piece, LANES), both...]
    all_to_all x1 -> x0, starting transfers between devices: 8.44 us -> none  [body(): got = lax.all_to_all(message, both, 0, 0, tiled=True)]
    unnamed x10 -> x7, local copies, waits for them, and re-layouts: 2.17 us -> 5.51 us
    another operation x5 -> x0, local copies, waits for them, and re-layouts: 2.46 us -> none  [the longest x4 1.57 us: pack(): jnp.stack(cut, axis=1).reshape(micro * local * tm, pairs * ROWS, LANES)]
    concatenate x2 -> x0, other arithmetic: 1.11 us -> none  [the longest x1 1.07 us: body(): message = jnp.concatenate([mine, top], axis=1)]
  transfers between devices with their start and end apart: 1 -> 0, of which waited for: 0 -> 0; matrix products, arithmetic and copies ran while one was open for 0% -> 0% of each run, Pallas kernels for 0% -> 0%
where the time goes in v2:
time: 65.6 us; the launch traced here: 65.4 us
  Pallas kernels  57.9 us (88%)
  local copies, waits for them, and re-layouts  6.89 us (11%)
  between operations  0.66 us (1%)
    pallas_call x1, Pallas kernels, body(): pl.pallas_call(functools.partial(kernel, sections, batches, tiles), out_s...  57.9 us
    unnamed x7, local copies, waits for them, and re-layouts  5.51 us
    broadcast_in_dim x2, local copies, waits for them, and re-layouts, body(): return (grad.reshape(acts.shape), kernels[None, :9], kernels[None, 9:])  1.38 us

profile of v2, /device:TPU:0, one launch (start us, length us, event | category | flops | bytes accessed | tf_op | source)
XLA Modules:
  0.0 65.4 jit_solution(1665038527694458606)
XLA Ops:
  0.6 0.0 copy-start
  0.6 2.1 %copy.7 = bf16[1,2,2,6,10240]{4,3,2,1,0:T(8,128)(2,1)} copy(bf16[1,2,2,6,10240]{4,2,3,1,0:T(2,128)(2,1)} %param.4) | data formatting | bytes 983040 | tf_op args[0]
  2.7 0.0 copy-done
  2.7 1.0 %copy.8 = bf16[2,2,6,10240]{3,2,1,0:T(8,128)(2,1)} copy(bf16[2,2,6,10240]{3,1,2,0:T(2,128)(2,1)S(1)} %copy-done) | data formatting | bytes 983040 | tf_op args[1]
  3.7 57.9 %shard_map.67 = (bf16[4,6,10240]{2,1,0:T(8,128)(2,1)}, f32[12,64,64]{2,1,0:T(8,128)}) custom-call(bf16[4,6,10240]{2,1,0:T(8,128)(2,1)} %bitcast.9, bf16[4,6,10240]{2,1,0:T(8,128)(2,1)} %bitcast.10, bf16[9,64,64]{2,1,0:T(8,128)(2,1)} %bitcast.12, bf16[3,64,64]{2,1,0:T(8,128)(2,1)} %bitcast.13), custom_call_target="tpu_custom_call" | custom-call | tf_op jit(solution)/shard_map/pallas_call | solution.py:321
  61.6 0.0 copy-start.1
  61.6 2.4 %copy.9 = bf16[1,2,2,6,10240]{4,2,3,1,0:T(2,128)(2,1)} copy(bf16[1,2,2,6,10240]{4,3,2,1,0:T(8,128)(2,1)} %bitcast.11) | data formatting | bytes 983040
  64.0 0.0 copy-done.1
  64.0 0.6 slice_bitcast_fusion.1
  64.7 0.7 %slice_bitcast_fusion = f32[1,9,64,64]{3,2,1,0:T(8,128)} fusion(f32[12,64,64]{2,1,0:T(8,128)S(1)} %copy-done.1), kind=kLoop, calls=%fused_computation | loop fusion | bytes 294912 | tf_op jit(solution)/shard_map/broadcast_in_dim | solution.py:358
Async XLA Ops:
  0.6 2.1 %copy-start = (bf16[2,2,6,10240]{3,1,2,0:T(2,128)(2,1)S(1)}, bf16[2,2,6,10240]{3,1,2,0:T(2,128)(2,1)}, u32[]{:S(2)}) copy-start(bf16[2,2,6,10240]{3,1,2,0:T(2,128)(2,1)} %param.5) | copy-start | bytes 1474564
  61.6 2.4 %copy-start.1 = (f32[12,64,64]{2,1,0:T(8,128)S(1)}, f32[12,64,64]{2,1,0:T(8,128)}, u32[]{:S(2)}) copy-start(f32[12,64,64]{2,1,0:T(8,128)} %get-tuple-element.6) | copy-start | bytes 589828

commit v3 on v2

--- a/solution.py
+++ b/solution.py
@@ -61,32 +61,37 @@
         time[:, at] = jnp.concatenate([jnp.concatenate(v, axis=1) for v in rows], axis=0)
 
 
-def pack(frame, stage, c, tiles):
-    tm, pairs = stage.shape[0], stage.shape[2] // ROWS
+def pack(frame, stage, c, tiles, line, skip):
+    tm, size = stage.shape[0], stage.shape[2]
     rows, width = frame.shape
     v = frame.astype(jnp.float32)
-    v = jnp.concatenate([v, jnp.zeros((ROWS - rows, width), jnp.float32)], axis=0)
-    zero = jnp.zeros((1, ROWS, LANES), jnp.float32)
-    cut = [v[:, LANES * p : LANES * (p + 1)][None] for p in range(width // LANES)]
-    cut = [zero] * HALO + cut + [zero] * pairs
+    for p in range(width // LANES):
+        at = (p + HALO) * rows
+        line[at : at + rows, :] = v[:, LANES * p : LANES * (p + 1)]
     for m in range(tm):
-        part = jnp.concatenate(cut[tiles * m : tiles * m + pairs], axis=0)
-        stage[m, c] = part.reshape(pairs * ROWS, LANES).astype(jnp.bfloat16)
+        at = (tiles * m + skip) * rows
+        stage[m, c] = line[at : at + size, :].astype(jnp.bfloat16)
+
+
+def spread(packed, loose, wide, rows, first, count):
+    loose[...] = packed.astype(jnp.float32)
+    for n in range(loose.shape[0]):
+        for p in range(count):
+            wide[n, first + p, 0:rows, :] = loose[n, rows * p : rows * (p + 1), :]
 
 
 def kernel(
-    sections, batches, tiles, acts, cot, ws_ref, wt_ref, out, grads,
+    sections, batches, tiles, acts, cot, ws_ref, wt_ref, out, spatial, temporal,
     x_stage, g_stage, x_buf, g_buf, r_buf, o_buf, home, fwd, back, time, acc, acc_t, ds,
     w_send, w_recv, w_piece, w_full,
+    line, x_loose, g_loose, o_loose, x_wide, g_wide,
     x_sem, g_sem, z_sem, o_sem, w_sem, f_sem,
 ):
     tm = x_stage.shape[0]
     chains, frame_rows, width = acts.shape
     chans = ws_ref.shape[-1]
-    ext = x_buf.shape[2]
-    pairs = ext // ROWS
+    pairs = x_wide.shape[1]
     tile_rows = o_buf.shape[2]
-    out_pairs = tile_rows // ROWS
     group = tm * batches
     section, me, core = [lax.axis_index(a) for a in ("section", "tm", "batch")]
     rank = me * batches + core
@@ -139,11 +144,15 @@
     def f_copy(e):
         return copy(w_piece, w_full.at[rank], f_sem, (e - 1,), member(e)[1])
 
-    pack(acts[0], x_stage, 0, tiles)
+    line[...] = jnp.zeros_like(line)
+    x_wide[...] = jnp.zeros_like(x_wide)
+    g_wide[...] = jnp.zeros_like(g_wide)
+    g_loose[...] = jnp.zeros_like(g_loose)
+    pack(acts[0], x_stage, 0, tiles, line, 0)
 
     @pl.when(section == sections - 1)
     def _():
-        pack(cot[0], g_stage, 0, tiles)
+        pack(cot[0], g_stage, 0, tiles, line, 1)
 
     more = (section > 0).astype(jnp.int32) + (section < sections - 1).astype(jnp.int32)
     pl.semaphore_wait(barrier, group - 1 + more)
@@ -151,11 +160,11 @@
     def send(c, carry):
         @pl.when(c > 0)
         def _():
-            pack(acts[c], x_stage, c, tiles)
+            pack(acts[c], x_stage, c, tiles, line, 0)
 
             @pl.when(section == sections - 1)
             def _():
-                pack(cot[c], g_stage, c, tiles)
+                pack(cot[c], g_stage, c, tiles, line, 1)
 
         for d in range(1, tm):
             x_copy(c, d).start()
@@ -181,7 +190,8 @@
     def turn(c, carry):
         for d in range(1, tm):
             x_copy(c, d).wait_recv()
-        x = x_buf[c].astype(jnp.float32).reshape(shape)
+        spread(x_buf[c], x_loose, x_wide, frame_rows, 0, pairs)
+        x = x_wide[...]
         xx = jnp.concatenate([x, neighbours(x)], axis=3)
         y = mm(flat(xx).astype(jnp.bfloat16), fwd[...], ((1,), (0,)))
         part = [y[:, LANES * i : LANES * (i + 1)].reshape(-1, ROWS, LANES) for i in range(3)]
@@ -200,7 +210,8 @@
         def _():
             z_copy(c).wait_recv()
 
-        g = g_buf[c].astype(jnp.float32).reshape(shape)
+        spread(g_buf[c], g_loose, g_wide, frame_rows, 1, pairs - 2)
+        g = g_wide[...]
         g3 = jnp.concatenate(
             [
                 jnp.concatenate([g[1:], blank], axis=0),
@@ -227,15 +238,18 @@
         row = lax.broadcasted_iota(jnp.int32, shape, 2)
         inside = (place >= 0) & (place < width // LANES) & (row < frame_rows)
         result = jnp.where(inside, g + inner, 0.0)
-        r_buf[c] = result.reshape(tm, ext, LANES).astype(jnp.bfloat16)
+        for n in range(tm):
+            for p in range(pairs - 2):
+                at = frame_rows * p
+                g_loose[n, at : at + frame_rows, :] = result[n, p + 1, 0:frame_rows]
+        r_buf[c] = g_loose[...].astype(jnp.bfloat16)
 
         @pl.when(section > 0)
         def _():
             z_copy(c).start()
 
-        o_buf[c] = (
-            result[:, HALO : HALO + out_pairs].reshape(tm, tile_rows, LANES).astype(jnp.bfloat16)
-        )
+        at = (HALO - 1) * frame_rows
+        o_buf[c] = g_loose[:, at : at + tile_rows, :].astype(jnp.bfloat16)
         for d in range(1, tm):
             o_copy(c, d).start()
         home[c, me] = o_buf[c, me]
@@ -260,9 +274,13 @@
     def unpack(c, carry):
         for d in range(1, tm):
             o_copy(c, d).wait_recv()
-        v = home[c].astype(jnp.float32).reshape(tm, out_pairs, ROWS, LANES)
-        cut = [v[m, p] for m in range(tm) for p in range(tiles)]
-        out[c] = jnp.concatenate(cut, axis=1)[:frame_rows].astype(jnp.bfloat16)
+        o_loose[...] = home[c].astype(jnp.float32)
+        cut = [
+            o_loose[m, frame_rows * p : frame_rows * (p + 1), :]
+            for m in range(tm)
+            for p in range(tiles)
+        ]
+        out[c] = jnp.concatenate(cut, axis=1).astype(jnp.bfloat16)
         return carry
 
     lax.fori_loop(0, chains - 1, unpack, 0)
@@ -280,7 +298,11 @@
         ds[k * rows : (k + 1) * rows, :] = w_full[k]
     for t in range(12):
         both = ds[(t // 2) * chans : (t // 2 + 1) * chans, :]
-        grads[t] = both[:, (t % 2) * chans : (t % 2 + 1) * chans]
+        half = both[:, (t % 2) * chans : (t % 2 + 1) * chans]
+        if t < 9:
+            spatial[t] = half
+        else:
+            temporal[t - 9] = half
 
     def finish(c, carry):
         for d in range(1, tm):
@@ -313,25 +335,25 @@
     tiles = width // LANES // tm
     pairs = tiles + 2 * HALO
     pairs += pairs % 2
-    ext = pairs * ROWS
-    tile_rows = tiles * ROWS + (tiles * ROWS) % 16
+    x_rows, g_rows, tile_rows = [-(-n * rows // 16) * 16 for n in (pairs, pairs - 2, tiles)]
     piece = 6 * chans // group
     bf16, f32 = jnp.bfloat16, jnp.float32
     vmem, dma = pltpu.VMEM, pltpu.SemaphoreType.DMA
-    grad, kernels = pl.pallas_call(
+    grad, spatial, temporal = pl.pallas_call(
         functools.partial(kernel, sections, batches, tiles),
         out_shape=[
             jax.ShapeDtypeStruct((chains, rows, width), bf16),
-            jax.ShapeDtypeStruct((12, chans, chans), f32),
+            jax.ShapeDtypeStruct((9, chans, chans), f32),
+            jax.ShapeDtypeStruct((3, chans, chans), f32),
         ],
         in_specs=[pl.BlockSpec(memory_space=vmem)] * 4,
-        out_specs=[pl.BlockSpec(memory_space=vmem)] * 2,
+        out_specs=[pl.BlockSpec(memory_space=vmem)] * 3,
         scratch_shapes=[
-            vmem((tm, chains, ext, LANES), bf16),
-            vmem((tm, chains, ext, LANES), bf16),
-            vmem((chains, tm, ext, LANES), bf16),
-            vmem((chains, tm, ext, LANES), bf16),
-            vmem((chains, tm, ext, LANES), bf16),
+            vmem((tm, chains, x_rows, LANES), bf16),
+            vmem((tm, chains, g_rows, LANES), bf16),
+            vmem((chains, tm, x_rows, LANES), bf16),
+            vmem((chains, tm, g_rows, LANES), bf16),
+            vmem((chains, tm, g_rows, LANES), bf16),
             vmem((chains, tm, tile_rows, LANES), bf16),
             vmem((chains, tm, tile_rows, LANES), bf16),
             vmem((2 * LANES, 3 * LANES), bf16),
@@ -344,6 +366,12 @@
             vmem((group, piece, LANES), bf16),
             vmem((piece, LANES), f32),
             vmem((group, piece, LANES), f32),
+            vmem(((width // LANES + HALO + pairs) * rows + 16, LANES), f32),
+            vmem((tm, x_rows, LANES), f32),
+            vmem((tm, g_rows, LANES), f32),
+            vmem((tm, tile_rows, LANES), f32),
+            vmem((tm, pairs, ROWS, LANES), f32),
+            vmem((tm, pairs, ROWS, LANES), f32),
             dma((2, chains, tm - 1)),
             dma((2, chains, tm - 1)),
             dma((2, chains)),
@@ -355,7 +383,7 @@
             collective_id=0, has_side_effects=True, vmem_limit_bytes=56 * 2**20
         ),
     )(acts.reshape(chains, rows, width), cot.reshape(chains, rows, width), spatial_weight[0], temporal_weight[0])
-    return grad.reshape(acts.shape), kernels[None, :9], kernels[None, 9:]
+    return grad.reshape(acts.shape), spatial[None], temporal[None]
 
 
 def solution(mesh):

time: 65.6 us -> 57.5 us (0.88)
  Pallas kernels: 57.9 us -> 49.5 us
    pallas_call x1, Pallas kernels: 57.9 us -> 49.5 us  [body(): pl.pallas_call(functools.partial(kernel, sections, batches, tiles), out_s...]
    unnamed x7 -> x11, local copies, waits for them, and re-layouts: 5.51 us -> 7.09 us
    broadcast_in_dim x2 -> x0, local copies, waits for them, and re-layouts: 1.38 us -> none  [body(): return (grad.reshape(acts.shape), kernels[None, :9], kernels[None, 9:])]
where the time goes in v3:
time: 57.5 us; the launch traced here: 57.3 us
  Pallas kernels  49.5 us (86%)
  local copies, waits for them, and re-layouts  7.09 us (12%)
  between operations  0.66 us (1%)
    pallas_call x1, Pallas kernels, body(): pl.pallas_call(functools.partial(kernel, sections, batches, tiles), out_s...  49.5 us
    unnamed x11, local copies, waits for them, and re-layouts  7.09 us

profile of v3, /device:TPU:0, one launch (start us, length us, event | category | flops | bytes accessed | tf_op | source)
XLA Modules:
  0.0 57.3 jit_solution(11210108538519389515)
XLA Ops:
  0.6 0.0 copy-start
  0.6 2.1 %copy.7 = bf16[1,2,2,6,10240]{4,3,2,1,0:T(8,128)(2,1)} copy(bf16[1,2,2,6,10240]{4,2,3,1,0:T(2,128)(2,1)} %param.4) | data formatting | bytes 983040 | tf_op args[0]
  2.7 0.0 copy-done
  2.7 1.0 %copy.8 = bf16[2,2,6,10240]{3,2,1,0:T(8,128)(2,1)} copy(bf16[2,2,6,10240]{3,1,2,0:T(2,128)(2,1)S(1)} %copy-done) | data formatting | bytes 983040 | tf_op args[1]
  3.7 49.5 %shard_map.67 = (bf16[4,6,10240]{2,1,0:T(8,128)(2,1)}, f32[9,64,64]{2,1,0:T(8,128)}, f32[3,64,64]{2,1,0:T(8,128)}) custom-call(bf16[4,6,10240]{2,1,0:T(8,128)(2,1)} %bitcast.7, bf16[4,6,10240]{2,1,0:T(8,128)(2,1)} %bitcast.8, bf16[9,64,64]{2,1,0:T(8,128)(2,1)} %bitcast.11, bf16[3,64,64]{2,1,0:T(8,128)(2,1)} %bitcast.13), custom_call_target="tpu_custom_call" | custom-call | tf_op jit(solution)/shard_map/pallas_call | solution.py:342
  53.2 0.0 copy-start.1
  53.2 2.4 %copy.9 = bf16[1,2,2,6,10240]{4,2,3,1,0:T(2,128)(2,1)} copy(bf16[1,2,2,6,10240]{4,3,2,1,0:T(8,128)(2,1)} %bitcast.9) | data formatting | bytes 983040
  55.7 0.0 copy-done.1
  55.7 0.0 copy-start.2
  55.7 0.7 %copy.12 = f32[1,9,64,64]{3,2,1,0:T(8,128)} copy(f32[1,9,64,64]{3,2,1,0:T(8,128)S(1)} %bitcast.10) | data formatting | bytes 294912
  56.4 0.2 copy-done.2
  56.6 0.6 %copy.13 = f32[1,3,64,64]{3,2,1,0:T(8,128)} copy(f32[1,3,64,64]{3,2,1,0:T(8,128)S(1)} %bitcast.12) | data formatting | bytes 98304
Async XLA Ops:
  0.6 2.1 %copy-start = (bf16[2,2,6,10240]{3,1,2,0:T(2,128)(2,1)S(1)}, bf16[2,2,6,10240]{3,1,2,0:T(2,128)(2,1)}, u32[]{:S(2)}) copy-start(bf16[2,2,6,10240]{3,1,2,0:T(2,128)(2,1)} %param.5) | copy-start | bytes 1474564
  53.2 2.4 %copy-start.1 = (f32[9,64,64]{2,1,0:T(8,128)S(1)}, f32[9,64,64]{2,1,0:T(8,128)}, u32[]{:S(2)}) copy-start(f32[9,64,64]{2,1,0:T(8,128)} %get-tuple-element.7) | copy-start | bytes 442372
  55.7 1.0 %copy-start.2 = (f32[3,64,64]{2,1,0:T(8,128)S(1)}, f32[3,64,64]{2,1,0:T(8,128)}, u32[]{:S(2)}) copy-start(f32[3,64,64]{2,1,0:T(8,128)} %get-tuple-element.8) | copy-start | bytes 147460

commit v4 on v3

--- a/solution.py
+++ b/solution.py
@@ -116,6 +116,18 @@
     def _():
         pl.semaphore_signal(barrier, inc=1, device_id=(section + 1, me, core), device_id_type=MESH)
 
+    @pl.when(section == sections - 1)
+    def _():
+        for d in range(1, tm):
+            device = (sections - 2, peer(d)[0], core)
+            pl.semaphore_signal(barrier, inc=1, device_id=device, device_id_type=MESH)
+
+    @pl.when(section == sections - 2)
+    def _():
+        for d in range(1, tm):
+            device = (sections - 1, peer(d)[0], core)
+            pl.semaphore_signal(barrier, inc=1, device_id=device, device_id_type=MESH)
+
     def copy(src, dst, sems, at, device):
         return pltpu.make_async_remote_copy(
             src_ref=src, dst_ref=dst, send_sem=sems.at[(0,) + at], recv_sem=sems.at[(1,) + at],
@@ -127,7 +139,8 @@
         return copy(x_stage.at[other, c], x_buf.at[c, me], x_sem, (c, d - 1), device)
 
     def g_copy(c, d):
-        other, device = peer(d)
+        other, _ = peer(d)
+        device = (sections - 1, other, core)
         return copy(g_stage.at[other, c], g_buf.at[c, me], g_sem, (c, d - 1), device)
 
     def z_copy(c):
@@ -150,11 +163,12 @@
     g_loose[...] = jnp.zeros_like(g_loose)
     pack(acts[0], x_stage, 0, tiles, line, 0)
 
-    @pl.when(section == sections - 1)
+    @pl.when(section >= sections - 2)
     def _():
         pack(cot[0], g_stage, 0, tiles, line, 1)
 
     more = (section > 0).astype(jnp.int32) + (section < sections - 1).astype(jnp.int32)
+    more += (section >= sections - 2).astype(jnp.int32) * (tm - 1)
     pl.semaphore_wait(barrier, group - 1 + more)
 
     def send(c, carry):
@@ -162,7 +176,7 @@
         def _():
             pack(acts[c], x_stage, c, tiles, line, 0)
 
-            @pl.when(section == sections - 1)
+            @pl.when(section >= sections - 2)
             def _():
                 pack(cot[c], g_stage, c, tiles, line, 1)
 
@@ -170,10 +184,13 @@
             x_copy(c, d).start()
         x_buf[c, me] = x_stage[me, c]
 
-        @pl.when(section == sections - 1)
+        @pl.when(section == sections - 1 - lax.rem(c, 2))
         def _():
             for d in range(1, tm):
                 g_copy(c, d).start()
+
+        @pl.when(section == sections - 1)
+        def _():
             g_buf[c, me] = g_stage[me, c]
 
         return carry
@@ -309,7 +326,7 @@
             x_copy(c, d).wait_send()
             o_copy(c, d).wait_send()
 
-        @pl.when(section == sections - 1)
+        @pl.when(section == sections - 1 - lax.rem(c, 2))
         def _():
             for d in range(1, tm):
                 g_copy(c, d).wait_send()

time: 57.5 us -> 61.7 us (1.073)
  Pallas kernels: 49.5 us -> 53.7 us
    pallas_call x1, Pallas kernels: 49.5 us -> 53.7 us  [body(): pl.pallas_call(functools.partial(kernel, sections, batches, tiles), out_s...]
where the time goes in v4:
time: 61.7 us; the launch traced here: 61.5 us
  Pallas kernels  53.7 us (87%)
  local copies, waits for them, and re-layouts  7.09 us (11%)
  between operations  0.66 us (1%)
    pallas_call x1, Pallas kernels, body(): pl.pallas_call(functools.partial(kernel, sections, batches, tiles), out_s...  53.7 us
    unnamed x11, local copies, waits for them, and re-layouts  7.09 us

profile of v4, /device:TPU:0, one launch (start us, length us, event | category | flops | bytes accessed | tf_op | source)
XLA Modules:
  0.0 61.5 jit_solution(8769367253455670276)
XLA Ops:
  0.6 0.0 copy-start
  0.6 2.1 %copy.7 = bf16[1,2,2,6,10240]{4,3,2,1,0:T(8,128)(2,1)} copy(bf16[1,2,2,6,10240]{4,2,3,1,0:T(2,128)(2,1)} %param.4) | data formatting | bytes 983040 | tf_op args[0]
  2.7 0.0 copy-done
  2.7 1.0 %copy.8 = bf16[2,2,6,10240]{3,2,1,0:T(8,128)(2,1)} copy(bf16[2,2,6,10240]{3,1,2,0:T(2,128)(2,1)S(1)} %copy-done) | data formatting | bytes 983040 | tf_op args[1]
  3.7 53.7 %shard_map.67 = (bf16[4,6,10240]{2,1,0:T(8,128)(2,1)}, f32[9,64,64]{2,1,0:T(8,128)}, f32[3,64,64]{2,1,0:T(8,128)}) custom-call(bf16[4,6,10240]{2,1,0:T(8,128)(2,1)} %bitcast.7, bf16[4,6,10240]{2,1,0:T(8,128)(2,1)} %bitcast.8, bf16[9,64,64]{2,1,0:T(8,128)(2,1)} %bitcast.11, bf16[3,64,64]{2,1,0:T(8,128)(2,1)} %bitcast.13), custom_call_target="tpu_custom_call" | custom-call | tf_op jit(solution)/shard_map/pallas_call | solution.py:359
  57.4 0.0 copy-start.1
  57.4 2.4 %copy.9 = bf16[1,2,2,6,10240]{4,2,3,1,0:T(2,128)(2,1)} copy(bf16[1,2,2,6,10240]{4,3,2,1,0:T(8,128)(2,1)} %bitcast.9) | data formatting | bytes 983040
  59.8 0.0 copy-done.1
  59.8 0.0 copy-start.2
  59.8 0.7 %copy.12 = f32[1,9,64,64]{3,2,1,0:T(8,128)} copy(f32[1,9,64,64]{3,2,1,0:T(8,128)S(1)} %bitcast.10) | data formatting | bytes 294912
  60.6 0.2 copy-done.2
  60.8 0.6 %copy.13 = f32[1,3,64,64]{3,2,1,0:T(8,128)} copy(f32[1,3,64,64]{3,2,1,0:T(8,128)S(1)} %bitcast.12) | data formatting | bytes 98304
Async XLA Ops:
  0.6 2.1 %copy-start = (bf16[2,2,6,10240]{3,1,2,0:T(2,128)(2,1)S(1)}, bf16[2,2,6,10240]{3,1,2,0:T(2,128)(2,1)}, u32[]{:S(2)}) copy-start(bf16[2,2,6,10240]{3,1,2,0:T(2,128)(2,1)} %param.5) | copy-start | bytes 1474564
  57.4 2.4 %copy-start.1 = (f32[9,64,64]{2,1,0:T(8,128)S(1)}, f32[9,64,64]{2,1,0:T(8,128)}, u32[]{:S(2)}) copy-start(f32[9,64,64]{2,1,0:T(8,128)} %get-tuple-element.7) | copy-start | bytes 442372
  59.8 1.0 %copy-start.2 = (f32[3,64,64]{2,1,0:T(8,128)S(1)}, f32[3,64,64]{2,1,0:T(8,128)}, u32[]{:S(2)}) copy-start(f32[3,64,64]{2,1,0:T(8,128)} %get-tuple-element.8) | copy-start | bytes 147460
